TPU v7x, 512 devices: a whole 4x4x16 slice. The times are simulated.
512 devices in a mesh: scan: 32 (over y, z_lo, core), det: 16 (over x, z_hi).
Axes of the slice: x: 4, y: 4, z: 16 (z_hi: 4, z_lo: 4; z = z_hi * 4 + z_lo), core: 2. Of those that a mesh axis runs over, the one named last changes fastest.
Arguments:
- intensities: float32 [64, 1024, 1024], P('det', 'scan'), may hold values from -6 to 6
- trotter_labels: int32 [64, 1024, 1024], P('det', 'scan'), may hold values from 0 to 2
- phase_shift: float32 [1024, 1024], P('scan'), may hold values from -3.140625 to 3.140625
Outputs:
- object_spectrum: float32 [2, 1024, 1024], P(None, 'scan', 'det')
Inputs may be any that keep to these rules, and one draw needn't show every extreme that they name: `trotter_labels`: 0: the pixel lies in neither aperture margin at that frequency; 1: in the left margin; 2: in the right margin.
All inputs are finite; a program needn't handle non-finite values.
Results may differ from a plain program's by a relative error of at most 0.0003.
Values sent between devices are 32-bit elements; how exact they have to be, the bound alone decides.
A program may use at most 64 MiB of HBM per device.

v0:
```python
import math

import jax
import jax.numpy as jnp
import ml_dtypes
import numpy as np
from jax import lax
from jax.experimental import pallas as pl
from jax.experimental.pallas import tpu as pltpu
from jax.sharding import PartitionSpec as P

MESH = pl.DeviceIdType.MESH
F32 = jnp.float32
BF16 = jnp.bfloat16

N = 1024
SCAN = 32
BLOCK = 32
PARTS = (0, 2, 1, 3)
ROWS = BLOCK // 4
PIX = 4
X = 4
Z = 4


def split_table(table):
    high = table.astype(ml_dtypes.bfloat16)
    low = (table - high.astype(np.float64)).astype(ml_dtypes.bfloat16)
    return high, low


def make_tables():
    index = np.arange(N)
    angles = (index[:, None] * index[None, :] % N) * (2.0 * math.pi / N)
    cosine, sine = np.cos(angles), np.sin(angles)
    cos_v = cosine[:, :256].reshape(SCAN, ROWS, 4, 256)
    sin_v = sine[:, :256].reshape(SCAN, ROWS, 4, 256)
    even, odd = [], []
    for v in PARTS:
        c, s = cos_v[:, :, v], sin_v[:, :, v]
        if v % 2 == 0:
            table = np.stack([c, -s], axis=1)
        else:
            sign = 1.0 if v == 3 else -1.0
            table = np.stack(
                [np.concatenate([c, sign * s], 2), np.concatenate([-s, sign * c], 2)], axis=1)
        table = np.concatenate(split_table(table.reshape(512, -1)), axis=0)
        (odd if v % 2 else even).append(table)
    twiddle = np.stack([cosine[:32, :32], sine[:32, :32]])
    twiddle = np.tile(twiddle, (1, 1, PIX)).astype(np.float32)[:, :, None]
    twiddle = np.repeat(twiddle, ROWS, axis=2)
    u2 = np.arange(32)
    lanes = ((u2 % 4) * 32 + u2 // 4)[None, :] + 8 * np.arange(PIX)[:, None]
    small = np.zeros((2, 128, 128))
    for k in range(PIX):
        for e, table in enumerate((cosine, sine)):
            small[e, k * 32:(k + 1) * 32, lanes[k]] = table[:32, 0:N:32].T
    row = np.block([[small[0], -small[1]], [small[1], small[0]]]) / (N * 8.0)
    row = np.stack(split_table(row))
    return np.stack(even), np.stack(odd), row, twiddle


def swap_bit(first, second, width):
    clear = lax.broadcasted_iota(jnp.int32, first.shape, 1) % (2 * width) < width
    return (
        jnp.where(clear, first, pltpu.roll(second, width, 1)),
        jnp.where(clear, pltpu.roll(first, 128 - width, 1), second),
    )


def swap_bits(parts, widths):
    parts = list(parts)
    step = len(parts)
    for width in widths:
        step //= 2
        for n in range(len(parts)):
            if n // step % 2 == 0:
                parts[n], parts[n + step] = swap_bit(parts[n], parts[n + step], width)
    return parts


def sum_blocks(parts):
    lane = lax.broadcasted_iota(jnp.int32, parts[0].shape, 1)
    for width in (16, 8):
        clear = lane % (2 * width) < width
        half = len(parts) // 2
        sums = []
        for one, two in zip(parts[:half], parts[half:]):
            other = jnp.where(clear, two, one)
            other = jnp.where(
                clear, pltpu.roll(other, 128 - width, 1), pltpu.roll(other, width, 1))
            sums.append(jnp.where(clear, one, two) + other)
        parts = sums
    return parts[0]


def four_points(p):
    (ar, ai), (br, bi), (cr, ci), (dr, di) = p
    sr, si, er, ei = ar + cr, ai + ci, ar - cr, ai - ci
    tr, ti, fr, fi = br + dr, bi + di, br - dr, bi - di
    return [(sr + tr, si + ti), (er + fi, ei - fr), (sr - tr, si - ti), (er - fi, ei + fr)]


def eight_points(p):
    root = math.sqrt(0.5)
    even = four_points(p[0::2])
    odd = four_points(p[1::2])
    (r1, i1), (r2, i2), (r3, i3) = odd[1:]
    odd[1] = ((r1 + i1) * root, (i1 - r1) * root)
    odd[2] = (i2, -r2)
    odd[3] = ((i3 - r3) * root, -(r3 + i3) * root)
    out = [(e[0] + o[0], e[1] + o[1]) for e, o in zip(even, odd)]
    return out + [(e[0] - o[0], e[1] - o[1]) for e, o in zip(even, odd)]


def turn(p, step):
    if step == 0:
        return p
    c, s = math.cos(2.0 * math.pi * step / 32), math.sin(2.0 * math.pi * step / 32)
    return p[0] * c + p[1] * s, p[1] * c - p[0] * s


def split3(value):
    high = value.astype(BF16)
    rest = value - high.astype(F32)
    middle = rest.astype(BF16)
    return high, middle, (rest - middle.astype(F32)).astype(BF16)


def kernel(
    x_hbm, lab_hbm, phase_hbm, even_hbm, odd_hbm, row_hbm, twiddle_hbm, o_ref,
    x_v, lab_v, phase_v, even_v, odd_v, row_v, twiddle_v,
    xt, sbuf, rbuf, mixed, turned, lhs, cos_v, sin_v,
    wr, wi, psend, precv, zsend, zrecv, o_v,
    in_sem, send_sem, recv_sem, psend_sem, precv_sem, zsend_sem, zrecv_sem,
):
    me = lax.axis_index("scan")
    det = lax.axis_index("det")
    x, z = det // Z, det % Z

    x_copy = pltpu.make_async_copy(x_hbm, x_v, in_sem.at[0])
    lab_copies = [
        pltpu.make_async_copy(
            lab_hbm.at[:, :, pl.ds(m * 128, 128)], lab_v.at[m], in_sem.at[1])
        for m in range(8)
    ]
    phase_copies = [
        pltpu.make_async_copy(phase_hbm.at[:, pl.ds(m * 128, 128)], phase_v.at[m], in_sem.at[2])
        for m in range(8)
    ]
    row_copy = pltpu.make_async_copy(row_hbm, row_v, in_sem.at[3])
    twiddle_copy = pltpu.make_async_copy(twiddle_hbm, twiddle_v, in_sem.at[4])
    col_copies = [
        pltpu.make_async_copy(table.at[p % 2], to.at[p % 2], in_sem.at[6 + p])
        for p, (table, to) in enumerate([(even_hbm, even_v)] * 2 + [(odd_hbm, odd_v)] * 2)
    ]

    x_copy.start()
    col_copies[0].start()

    barrier = pltpu.get_barrier_semaphore()

    @pl.loop(1, SCAN)
    def _(i):
        pl.semaphore_signal(
            barrier, inc=1, device_id=(lax.rem(me + i, SCAN), det), device_id_type=MESH)

    for i in range(1, 4):
        pl.semaphore_signal(
            barrier, inc=1, device_id=(me, lax.rem(x + i, X) * Z + z), device_id_type=MESH)
        pl.semaphore_signal(
            barrier, inc=1, device_id=(me, x * Z + lax.rem(z + i, Z)), device_id_type=MESH)

    for p in range(1, 4):
        col_copies[p].start()
    for copy in lab_copies + phase_copies:
        copy.start()
    row_copy.start()
    twiddle_copy.start()

    x_copy.wait()
    quarter = [[x_v[:, :, q * 256 + h * 128:q * 256 + (h + 1) * 128].reshape(128, 128)
                for q in range(4)] for h in range(2)]

    def put(value, at):
        value = jnp.transpose(value)
        high = value.astype(BF16)
        xt[at:at + 128, :128] = high
        xt[at:at + 128, 128:] = (value - high.astype(F32)).astype(BF16)

    for h, (x0, x1, x2, x3) in enumerate(quarter):
        put((x0 + x2) + (x1 + x3), h * 128)

    def column_part(p):
        col_copies[p].wait()
        table = even_v if p < 2 else odd_v
        rows = xt[p * 256:(p + 1) * 256] if p < 2 else xt[512:]
        prod = jnp.dot(table[p % 2], rows, preferred_element_type=F32)
        top = prod[:512] + prod[512:]
        sbuf[p] = (top[:, :128] + top[:, 128:]).reshape(SCAN, 2, ROWS, 128)

    column_part(0)
    for h, (x0, x1, x2, x3) in enumerate(quarter):
        put((x0 + x2) - (x1 + x3), 256 + h * 128)
    column_part(1)
    for h, (x0, x1, x2, x3) in enumerate(quarter):
        put(x0 - x2, 512 + h * 128)
        put(x1 - x3, 768 + h * 128)
    column_part(2)
    column_part(3)

    pl.semaphore_wait(barrier, SCAN - 1 + X - 1 + Z - 1)
    chip = lax.div(me, 2)

    @pl.loop(0, 8)
    def _(n):
        p, core = lax.div(n, 2), lax.rem(n, 2)

        @pl.loop(1, 17)
        def _(i):
            to = lax.rem(chip + i, 16) * 2 + core

            @pl.when(to != me)
            def _():
                pltpu.make_async_remote_copy(
                    src_ref=sbuf.at[p, to],
                    dst_ref=rbuf.at[p, me],
                    send_sem=send_sem,
                    recv_sem=recv_sem.at[p],
                    device_id=(to, det),
                    device_id_type=MESH,
                ).start()

    for p in range(4):
        rbuf[p, me] = sbuf[p, me]

    pltpu.make_async_copy(phase_v, phase_v, in_sem.at[2]).wait()
    cos_v[...] = jnp.cos(phase_v[...])
    sin_v[...] = jnp.sin(phase_v[...])
    pltpu.make_async_copy(lab_v, lab_v, in_sem.at[1]).wait()
    for p, v in enumerate(PARTS):
        reals, imags = [], []
        for k in range(PIX):
            for m in range(8):
                cosine = cos_v[m, pl.ds(v, ROWS, stride=4), :]
                sine = sin_v[m, pl.ds(v, ROWS, stride=4), :]
                zero = jnp.zeros_like(cosine)
                labels = lab_v[m, k, pl.ds(v, ROWS, stride=4), :]
                left = labels == 1
                right = labels == 2
                reals.append(jnp.where(left, cosine, jnp.where(right, -cosine, zero)))
                imags.append(jnp.where(jnp.logical_or(left, right), -sine, zero))
        for to, parts in ((wr, reals), (wi, imags)):
            for u1, part in enumerate(swap_bits(parts, (16, 8, 4, 2, 1))):
                to[p, u1] = part

    row_copy.wait()
    twiddle_copy.wait()

    def row_part(p):
        most = rbuf.at[p, pl.ds(0, SCAN - 1)]
        pltpu.make_async_copy(most, most, recv_sem.at[p]).wait()
        for e in range(4):
            points = [(rbuf[p, 4 * g + e, 0], rbuf[p, 4 * g + e, 1]) for g in range(8)]
            for b, point in enumerate(eight_points(points)):
                mixed[e, b, 0], mixed[e, b, 1] = turn(point, e * b)
        for b in range(8):
            points = four_points([(mixed[e, b, 0], mixed[e, b, 1]) for e in range(4)])
            for c, (re, im) in enumerate(points):
                u1 = b + 8 * c
                cosine, sine = twiddle_v[0, u1], twiddle_v[1, u1]
                turned[u1 * ROWS:(u1 + 1) * ROWS, :128] = re * cosine + im * sine
                turned[u1 * ROWS:(u1 + 1) * ROWS, 128:] = im * cosine - re * sine
        for qh in range(2):
            value = turned[qh * 128:(qh + 1) * 128]
            high = value.astype(BF16)
            lhs[qh, :128] = high
            lhs[qh, 128:] = (value - high.astype(F32)).astype(BF16)
            both = jnp.dot(lhs[qh], row_v[0], preferred_element_type=F32)
            low = jnp.dot(lhs[qh, :128], row_v[1], preferred_element_type=F32)
            spec = both[:128] + both[128:] + low
            sums = [], []
            for ql in range(4):
                reals, imags = [], []
                for e in range(4):
                    at = ql * 4 + e
                    re = spec[at * ROWS:(at + 1) * ROWS, :128]
                    im = spec[at * ROWS:(at + 1) * ROWS, 128:]
                    w_re, w_im = wr[p, qh * 16 + at], wi[p, qh * 16 + at]
                    reals.append(re * w_re - im * w_im)
                    imags.append(re * w_im + im * w_re)
                sums[0].append(sum_blocks(reals))
                sums[1].append(sum_blocks(imags))
            for e in range(2):
                for q, part in enumerate(swap_bits(sums[e], (4, 2))):
                    psend[p, q, qh, e] = part

        @pl.loop(1, X)
        def _(j):
            q = (x + j) % X
            pltpu.make_async_remote_copy(
                src_ref=psend.at[p, q],
                dst_ref=precv.at[p, j - 1],
                send_sem=psend_sem.at[p],
                recv_sem=precv_sem.at[p],
                device_id=(me, q * Z + z),
                device_id_type=MESH,
            ).start()

    def sum_x(p):
        pltpu.make_async_copy(precv.at[p], precv.at[p], precv_sem.at[p]).wait()
        parts = []
        for qh in range(2):
            for e in range(2):
                total = psend[p, x, qh, e]
                for j in range(X - 1):
                    total = total + precv[p, j, qh, e]
                parts.append(total)
        for h, part in enumerate(swap_bits(parts, (1, 64))):
            zsend[p, h] = part

        @pl.loop(1, Z)
        def _(j):
            to = (z + j) % Z
            pltpu.make_async_remote_copy(
                src_ref=zsend.at[p, to],
                dst_ref=zrecv.at[p, j - 1],
                send_sem=zsend_sem.at[p],
                recv_sem=zrecv_sem.at[p],
                device_id=(me, x * Z + to),
                device_id_type=MESH,
            ).start()

    @pl.loop(0, 4)
    def _(p):
        @pl.when(p > 0)
        def _():
            sum_x(p - 1)

        row_part(p)

    sum_x(3)

    lane = lax.broadcasted_iota(jnp.int32, (128, 128), 0)
    target = (
        lane // 32 * 32 + (lane % 2 * 4 + lane // 2 % 4) * 4 + lane // 8 % 4)
    order = jnp.where(
        target == lax.broadcasted_iota(jnp.int32, (128, 128), 1), 1.0, 0.0).astype(BF16)
    results = []
    for p in range(4):
        pltpu.make_async_copy(zrecv.at[p], zrecv.at[p], zrecv_sem.at[p]).wait()
        results.append(zsend[p, z] + zrecv[p, 0] + zrecv[p, 1] + zrecv[p, 2])
    result = jnp.concatenate(results, axis=0)
    moved = jnp.dot(jnp.concatenate(split3(result), axis=0), order, preferred_element_type=F32)
    result = moved[:BLOCK] + moved[BLOCK:2 * BLOCK] + moved[2 * BLOCK:]
    other = pltpu.roll(result, 64, 1)
    for p, v in enumerate(PARTS):
        o_v[0, pl.ds(v, ROWS, stride=4), :] = result[p * ROWS:(p + 1) * ROWS]
        o_v[1, pl.ds(v, ROWS, stride=4), :] = other[p * ROWS:(p + 1) * ROWS]
    o_ref[...] = o_v[:, :, :N // (X * Z)]

    for p in range(4):
        most = rbuf.at[p, pl.ds(0, SCAN - 1)]
        pltpu.make_async_copy(most, most, send_sem).wait()
        pltpu.make_async_copy(precv.at[p], precv.at[p], psend_sem.at[p]).wait()
        pltpu.make_async_copy(zrecv.at[p], zrecv.at[p], zsend_sem.at[p]).wait()


def local(even, odd, row, twiddle, intensities, trotter_labels, phase_shift):
    any_spec = pl.BlockSpec(memory_space=pl.ANY)
    dma = pltpu.SemaphoreType.DMA
    return pl.pallas_call(
        kernel,
        out_shape=jax.ShapeDtypeStruct((2, BLOCK, N // (X * Z)), F32),
        in_specs=[any_spec] * 7,
        out_specs=pl.BlockSpec(memory_space=pltpu.VMEM),
        scratch_shapes=[
            pltpu.VMEM((PIX, BLOCK, N), F32),
            pltpu.VMEM((8, PIX, BLOCK, 128), jnp.int32),
            pltpu.VMEM((8, BLOCK, 128), F32),
            pltpu.VMEM((2, 1024, 256), BF16),
            pltpu.VMEM((2, 1024, 512), BF16),
            pltpu.VMEM((2, 256, 256), BF16),
            pltpu.VMEM((2, 32, ROWS, 128), F32),
            pltpu.VMEM((N, 256), BF16),
            pltpu.VMEM((4, SCAN, 2, ROWS, 128), F32),
            pltpu.VMEM((4, SCAN, 2, ROWS, 128), F32),
            pltpu.VMEM((4, 8, 2, ROWS, 128), F32),
            pltpu.VMEM((256, 256), F32),
            pltpu.VMEM((2, 256, 256), BF16),
            pltpu.VMEM((8, BLOCK, 128), F32),
            pltpu.VMEM((8, BLOCK, 128), F32),
            pltpu.VMEM((4, 32, ROWS, 128), F32),
            pltpu.VMEM((4, 32, ROWS, 128), F32),
            pltpu.VMEM((4, X, 2, 2, ROWS, 128), F32),
            pltpu.VMEM((4, X - 1, 2, 2, ROWS, 128), F32),
            pltpu.VMEM((4, Z, ROWS, 128), F32),
            pltpu.VMEM((4, Z - 1, ROWS, 128), F32),
            pltpu.VMEM((2, BLOCK, 128), F32),
            dma((10,)),
            dma,
            dma((4,)),
            dma((4,)),
            dma((4,)),
            dma((4,)),
            dma((4,)),
        ],
        compiler_params=pltpu.CompilerParams(
            collective_id=0, has_side_effects=True, vmem_limit_bytes=55140 * 1024),
        name="ptycho",
    )(intensities, trotter_labels, phase_shift, even, odd, row, twiddle)


def solution(mesh):
    tables = make_tables()
    placed = (P("det", "scan", None), P("det", "scan", None), P("scan", None))
    fixed = tuple(P(*[None] * table.ndim) for table in tables)
    mapped = jax.shard_map(
        local, mesh=mesh, in_specs=fixed + placed, out_specs=P(None, "scan", "det"),
        check_vma=False)

    def run(intensities, trotter_labels, phase_shift):
        return mapped(*map(jnp.asarray, tables), intensities, trotter_labels, phase_shift)

    return run
```

profile of v0, /device:TPU:1, one launch (start us, length us, event | category | flops | bytes accessed | tf_op | source)
XLA Modules:
  0.0 54.1 jit_solution(3580431298781288906)
XLA Ops:
  0.0 53.4 %ptycho.1 = f32[2,32,64]{2,1,0:T(8,128)S(1)} custom-call(f32[4,32,1024]{2,1,0:T(8,128)} %x_hbm.1, s32[4,32,1024]{2,1,0:T(8,128)} %lab_hbm.1, f32[32,1024]{1,0:T(8,128)} %phase_hbm.1, bf16[2,1024,256]{2,1,0:T(8,128)(2,1)} %constant.8.clone.even_hbm, bf16[2,1024,512]{2,1,0:T(8,128)(2,1)} %constant.9.clone.odd_hbm, ...), custom_call_target="tpu_custom_call" | custom-call | tf_op jit(solution)/shard_map/ptycho/pallas_call | solution.py:372
  53.5 0.6 %copy.9 = f32[2,32,64]{2,1,0:T(8,128)} copy(f32[2,32,64]{2,1,0:T(8,128)S(1)} %ptycho.1) | data formatting | bytes 32768
where the time goes:
time: 54.2 us; the launch traced here: 54.1 us
  Pallas kernels  53.4 us (99%)
  local copies, waits for them, and re-layouts  0.62 us (1%)
    pallas_call x1, Pallas kernels, local(): pl.pallas_call(kernel, out_shape=jax.ShapeDtypeStruct((2, BLOCK, N // (X...  53.4 us

commit v1 on v0

--- a/solution.py
+++ b/solution.py
@@ -160,8 +160,7 @@
 
     barrier = pltpu.get_barrier_semaphore()
 
-    @pl.loop(1, SCAN)
-    def _(i):
+    for i in range(1, SCAN):
         pl.semaphore_signal(
             barrier, inc=1, device_id=(lax.rem(me + i, SCAN), det), device_id_type=MESH)
 
@@ -212,25 +211,28 @@
     pl.semaphore_wait(barrier, SCAN - 1 + X - 1 + Z - 1)
     chip = lax.div(me, 2)
 
-    @pl.loop(0, 8)
-    def _(n):
-        p, core = lax.div(n, 2), lax.rem(n, 2)
-
-        @pl.loop(1, 17)
+    def send_part(p):
+        @pl.loop(0, 32)
         def _(i):
-            to = lax.rem(chip + i, 16) * 2 + core
+            to = lax.rem(chip + 1 + lax.rem(i, 16), 16) * 2 + lax.div(i, 16)
 
             @pl.when(to != me)
             def _():
                 pltpu.make_async_remote_copy(
                     src_ref=sbuf.at[p, to],
                     dst_ref=rbuf.at[p, me],
-                    send_sem=send_sem,
+                    send_sem=send_sem.at[p],
                     recv_sem=recv_sem.at[p],
                     device_id=(to, det),
                     device_id_type=MESH,
                 ).start()
 
+    def wait_sent(p):
+        most = rbuf.at[p, pl.ds(0, SCAN - 1)]
+        pltpu.make_async_copy(most, most, send_sem.at[p]).wait()
+
+    send_part(0)
+    send_part(1)
     for p in range(4):
         rbuf[p, me] = sbuf[p, me]
 
@@ -333,6 +335,11 @@
 
     @pl.loop(0, 4)
     def _(p):
+        @pl.when(p < 2)
+        def _():
+            wait_sent(p)
+            send_part(p + 2)
+
         @pl.when(p > 0)
         def _():
             sum_x(p - 1)
@@ -360,8 +367,8 @@
     o_ref[...] = o_v[:, :, :N // (X * Z)]
 
     for p in range(4):
-        most = rbuf.at[p, pl.ds(0, SCAN - 1)]
-        pltpu.make_async_copy(most, most, send_sem).wait()
+        if p >= 2:
+            wait_sent(p)
         pltpu.make_async_copy(precv.at[p], precv.at[p], psend_sem.at[p]).wait()
         pltpu.make_async_copy(zrecv.at[p], zrecv.at[p], zsend_sem.at[p]).wait()
 
@@ -398,7 +405,7 @@
             pltpu.VMEM((4, Z - 1, ROWS, 128), F32),
             pltpu.VMEM((2, BLOCK, 128), F32),
             dma((10,)),
-            dma,
+            dma((4,)),
             dma((4,)),
             dma((4,)),
             dma((4,)),

time: 54.2 us -> 54.1 us (level)
  no operation moved by 1% of the time
where the time goes in v1:
time: 54.1 us; the launch traced here: 54 us
  Pallas kernels  53.3 us (99%)
  local copies, waits for them, and re-layouts  0.62 us (1%)
    pallas_call x1, Pallas kernels, local(): pl.pallas_call(kernel, out_shape=jax.ShapeDtypeStruct((2, BLOCK, N // (X...  53.3 us

profile of v1, /device:TPU:1, one launch (start us, length us, event | category | flops | bytes accessed | tf_op | source)
XLA Modules:
  0.0 54.0 jit_solution(1451011987427078363)
XLA Ops:
  0.0 53.3 %ptycho.1 = f32[2,32,64]{2,1,0:T(8,128)S(1)} custom-call(f32[4,32,1024]{2,1,0:T(8,128)} %x_hbm.1, s32[4,32,1024]{2,1,0:T(8,128)} %lab_hbm.1, f32[32,1024]{1,0:T(8,128)} %phase_hbm.1, bf16[2,1024,256]{2,1,0:T(8,128)(2,1)} %constant.8.clone.even_hbm, bf16[2,1024,512]{2,1,0:T(8,128)(2,1)} %constant.9.clone.odd_hbm, ...), custom_call_target="tpu_custom_call" | custom-call | tf_op jit(solution)/shard_map/ptycho/pallas_call | solution.py:379
  53.4 0.6 %copy.9 = f32[2,32,64]{2,1,0:T(8,128)} copy(f32[2,32,64]{2,1,0:T(8,128)S(1)} %ptycho.1) | data formatting | bytes 32768

commit v2 on v1

--- a/solution.py
+++ b/solution.py
@@ -198,17 +198,6 @@
         top = prod[:512] + prod[512:]
         sbuf[p] = (top[:, :128] + top[:, 128:]).reshape(SCAN, 2, ROWS, 128)
 
-    column_part(0)
-    for h, (x0, x1, x2, x3) in enumerate(quarter):
-        put((x0 + x2) - (x1 + x3), 256 + h * 128)
-    column_part(1)
-    for h, (x0, x1, x2, x3) in enumerate(quarter):
-        put(x0 - x2, 512 + h * 128)
-        put(x1 - x3, 768 + h * 128)
-    column_part(2)
-    column_part(3)
-
-    pl.semaphore_wait(barrier, SCAN - 1 + X - 1 + Z - 1)
     chip = lax.div(me, 2)
 
     def send_part(p):
@@ -231,8 +220,18 @@
         most = rbuf.at[p, pl.ds(0, SCAN - 1)]
         pltpu.make_async_copy(most, most, send_sem.at[p]).wait()
 
+    column_part(0)
+    pl.semaphore_wait(barrier, SCAN - 1 + X - 1 + Z - 1)
     send_part(0)
+    for h, (x0, x1, x2, x3) in enumerate(quarter):
+        put((x0 + x2) - (x1 + x3), 256 + h * 128)
+    column_part(1)
     send_part(1)
+    for h, (x0, x1, x2, x3) in enumerate(quarter):
+        put(x0 - x2, 512 + h * 128)
+        put(x1 - x3, 768 + h * 128)
+    column_part(2)
+    column_part(3)
     for p in range(4):
         rbuf[p, me] = sbuf[p, me]
 

time: 54.1 us -> 53.7 us (level)
  no operation moved by 1% of the time
where the time goes in v2:
time: 53.7 us; the launch traced here: 53.6 us
  Pallas kernels  53 us (99%)
  local copies, waits for them, and re-layouts  0.62 us (1%)
    pallas_call x1, Pallas kernels, local(): pl.pallas_call(kernel, out_shape=jax.ShapeDtypeStruct((2, BLOCK, N // (X...  53 us

profile of v2, /device:TPU:1, one launch (start us, length us, event | category | flops | bytes accessed | tf_op | source)
XLA Modules:
  0.0 53.6 jit_solution(17431847352414466468)
XLA Ops:
  0.0 53.0 %ptycho.1 = f32[2,32,64]{2,1,0:T(8,128)S(1)} custom-call(f32[4,32,1024]{2,1,0:T(8,128)} %x_hbm.1, s32[4,32,1024]{2,1,0:T(8,128)} %lab_hbm.1, f32[32,1024]{1,0:T(8,128)} %phase_hbm.1, bf16[2,1024,256]{2,1,0:T(8,128)(2,1)} %constant.8.clone.even_hbm, bf16[2,1024,512]{2,1,0:T(8,128)(2,1)} %constant.9.clone.odd_hbm, ...), custom_call_target="tpu_custom_call" | custom-call | tf_op jit(solution)/shard_map/ptycho/pallas_call | solution.py:378
  53.0 0.6 %copy.9 = f32[2,32,64]{2,1,0:T(8,128)} copy(f32[2,32,64]{2,1,0:T(8,128)S(1)} %ptycho.1) | data formatting | bytes 32768

commit v3 on v2

--- a/solution.py
+++ b/solution.py
@@ -198,35 +198,41 @@
         top = prod[:512] + prod[512:]
         sbuf[p] = (top[:, :128] + top[:, 128:]).reshape(SCAN, 2, ROWS, 128)
 
-    chip = lax.div(me, 2)
-
-    def send_part(p):
-        @pl.loop(0, 32)
+    chip, own = lax.div(me, 2), lax.rem(me, 2)
+
+    def send_chunk(q):
+        p, core = lax.div(q, 2), lax.rem(q, 2)
+
+        @pl.loop(1, 17)
         def _(i):
-            to = lax.rem(chip + 1 + lax.rem(i, 16), 16) * 2 + lax.div(i, 16)
+            to = lax.rem(chip + i, 16) * 2 + core
 
             @pl.when(to != me)
             def _():
                 pltpu.make_async_remote_copy(
                     src_ref=sbuf.at[p, to],
                     dst_ref=rbuf.at[p, me],
-                    send_sem=send_sem.at[p],
+                    send_sem=send_sem.at[q],
                     recv_sem=recv_sem.at[p],
                     device_id=(to, det),
                     device_id_type=MESH,
                 ).start()
 
-    def wait_sent(p):
-        most = rbuf.at[p, pl.ds(0, SCAN - 1)]
-        pltpu.make_async_copy(most, most, send_sem.at[p]).wait()
+    def wait_sent(q):
+        same = lax.rem(q, 2) == own
+        for mine, count in ((same, 15), (jnp.logical_not(same), 16)):
+            @pl.when(mine)
+            def _(count=count):
+                most = rbuf.at[0, pl.ds(0, count)]
+                pltpu.make_async_copy(most, most, send_sem.at[q]).wait()
 
     column_part(0)
     pl.semaphore_wait(barrier, SCAN - 1 + X - 1 + Z - 1)
-    send_part(0)
+    send_chunk(0)
+    send_chunk(1)
     for h, (x0, x1, x2, x3) in enumerate(quarter):
         put((x0 + x2) - (x1 + x3), 256 + h * 128)
     column_part(1)
-    send_part(1)
     for h, (x0, x1, x2, x3) in enumerate(quarter):
         put(x0 - x2, 512 + h * 128)
         put(x1 - x3, 768 + h * 128)
@@ -332,19 +338,24 @@
                 device_id_type=MESH,
             ).start()
 
-    @pl.loop(0, 4)
-    def _(p):
-        @pl.when(p < 2)
+    @pl.loop(0, 8)
+    def _(q):
+        p = lax.div(q, 2)
+
+        @pl.when(q < 6)
         def _():
-            wait_sent(p)
-            send_part(p + 2)
-
-        @pl.when(p > 0)
+            wait_sent(q)
+            send_chunk(q + 2)
+
+        @pl.when(lax.rem(q, 2) == 1)
         def _():
-            sum_x(p - 1)
-
-        row_part(p)
-
+            @pl.when(jnp.logical_and(p > 0, p < 3))
+            def _():
+                sum_x(p - 1)
+
+            row_part(p)
+
+    sum_x(2)
     sum_x(3)
 
     lane = lax.broadcasted_iota(jnp.int32, (128, 128), 0)
@@ -366,8 +377,8 @@
     o_ref[...] = o_v[:, :, :N // (X * Z)]
 
     for p in range(4):
-        if p >= 2:
-            wait_sent(p)
+        if p < 2:
+            wait_sent(6 + p)
         pltpu.make_async_copy(precv.at[p], precv.at[p], psend_sem.at[p]).wait()
         pltpu.make_async_copy(zrecv.at[p], zrecv.at[p], zsend_sem.at[p]).wait()
 
@@ -404,7 +415,7 @@
             pltpu.VMEM((4, Z - 1, ROWS, 128), F32),
             pltpu.VMEM((2, BLOCK, 128), F32),
             dma((10,)),
-            dma((4,)),
+            dma((8,)),
             dma((4,)),
             dma((4,)),
             dma((4,)),

time: 53.7 us -> 53.3 us (level)
  no operation moved by 1% of the time
where the time goes in v3:
time: 53.3 us; the launch traced here: 53.1 us
  Pallas kernels  52.5 us (98%)
  local copies, waits for them, and re-layouts  0.62 us (1%)
    pallas_call x1, Pallas kernels, local(): pl.pallas_call(kernel, out_shape=jax.ShapeDtypeStruct((2, BLOCK, N // (X...  52.5 us

profile of v3, /device:TPU:1, one launch (start us, length us, event | category | flops | bytes accessed | tf_op | source)
XLA Modules:
  0.0 53.1 jit_solution(9515250670268884052)
XLA Ops:
  0.0 52.5 %ptycho.1 = f32[2,32,64]{2,1,0:T(8,128)S(1)} custom-call(f32[4,32,1024]{2,1,0:T(8,128)} %x_hbm.1, s32[4,32,1024]{2,1,0:T(8,128)} %lab_hbm.1, f32[32,1024]{1,0:T(8,128)} %phase_hbm.1, bf16[2,1024,256]{2,1,0:T(8,128)(2,1)} %constant.8.clone.even_hbm, bf16[2,1024,512]{2,1,0:T(8,128)(2,1)} %constant.9.clone.odd_hbm, ...), custom_call_target="tpu_custom_call" | custom-call | tf_op jit(solution)/shard_map/ptycho/pallas_call | solution.py:389
  52.5 0.6 %copy.9 = f32[2,32,64]{2,1,0:T(8,128)} copy(f32[2,32,64]{2,1,0:T(8,128)S(1)} %ptycho.1) | data formatting | bytes 32768

commit v4 on v3

--- a/solution.py
+++ b/solution.py
@@ -21,6 +21,7 @@
 PIX = 4
 X = 4
 Z = 4
+FIRST = 1
 
 
 def split_table(table):
@@ -200,23 +201,31 @@
 
     chip, own = lax.div(me, 2), lax.rem(me, 2)
 
+    def send(p, to, q):
+        pltpu.make_async_remote_copy(
+            src_ref=sbuf.at[p, to],
+            dst_ref=rbuf.at[p, me],
+            send_sem=send_sem.at[jnp.minimum(q, 6)],
+            recv_sem=recv_sem.at[p],
+            device_id=(to, det),
+            device_id_type=MESH,
+        ).start()
+
     def send_chunk(q):
         p, core = lax.div(q, 2), lax.rem(q, 2)
+
+        @pl.when(jnp.logical_and(q == 6, me != FIRST))
+        def _():
+            send(p, FIRST, q)
 
         @pl.loop(1, 17)
         def _(i):
             to = lax.rem(chip + i, 16) * 2 + core
-
-            @pl.when(to != me)
+            led = jnp.logical_and(p == 3, to == FIRST)
+
+            @pl.when(jnp.logical_not(jnp.logical_or(to == me, led)))
             def _():
-                pltpu.make_async_remote_copy(
-                    src_ref=sbuf.at[p, to],
-                    dst_ref=rbuf.at[p, me],
-                    send_sem=send_sem.at[q],
-                    recv_sem=recv_sem.at[p],
-                    device_id=(to, det),
-                    device_id_type=MESH,
-                ).start()
+                send(p, to, q)
 
     def wait_sent(q):
         same = lax.rem(q, 2) == own
@@ -377,8 +386,9 @@
     o_ref[...] = o_v[:, :, :N // (X * Z)]
 
     for p in range(4):
-        if p < 2:
-            wait_sent(6 + p)
+        if p == 0:
+            most = rbuf.at[0, pl.ds(0, SCAN - 1)]
+            pltpu.make_async_copy(most, most, send_sem.at[6]).wait()
         pltpu.make_async_copy(precv.at[p], precv.at[p], psend_sem.at[p]).wait()
         pltpu.make_async_copy(zrecv.at[p], zrecv.at[p], zsend_sem.at[p]).wait()
 
@@ -415,7 +425,7 @@
             pltpu.VMEM((4, Z - 1, ROWS, 128), F32),
             pltpu.VMEM((2, BLOCK, 128), F32),
             dma((10,)),
-            dma((8,)),
+            dma((7,)),
             dma((4,)),
             dma((4,)),
             dma((4,)),

time: 53.3 us -> 52.1 us (0.977)
  Pallas kernels: 52.5 us -> 51.1 us
    pallas_call x1, Pallas kernels: 52.5 us -> 51.1 us  [local(): pl.pallas_call(kernel, out_shape=jax.ShapeDtypeStruct((2, BLOCK, N // (X...]
where the time goes in v4:
time: 52.1 us; the launch traced here: 51.7 us
  Pallas kernels  51.1 us (98%)
  local copies, waits for them, and re-layouts  0.62 us (1%)
    pallas_call x1, Pallas kernels, local(): pl.pallas_call(kernel, out_shape=jax.ShapeDtypeStruct((2, BLOCK, N // (X...  51.1 us

profile of v4, /device:TPU:1, one launch (start us, length us, event | category | flops | bytes accessed | tf_op | source)
XLA Modules:
  0.0 51.7 jit_solution(17590494007681950895)
XLA Ops:
  0.0 51.1 %ptycho.1 = f32[2,32,64]{2,1,0:T(8,128)S(1)} custom-call(f32[4,32,1024]{2,1,0:T(8,128)} %x_hbm.1, s32[4,32,1024]{2,1,0:T(8,128)} %lab_hbm.1, f32[32,1024]{1,0:T(8,128)} %phase_hbm.1, bf16[2,1024,256]{2,1,0:T(8,128)(2,1)} %constant.8.clone.even_hbm, bf16[2,1024,512]{2,1,0:T(8,128)(2,1)} %constant.9.clone.odd_hbm, ...), custom_call_target="tpu_custom_call" | custom-call | tf_op jit(solution)/shard_map/ptycho/pallas_call | solution.py:399
  51.1 0.6 %copy.9 = f32[2,32,64]{2,1,0:T(8,128)} copy(f32[2,32,64]{2,1,0:T(8,128)S(1)} %ptycho.1) | data formatting | bytes 32768

commit v5 on v4

--- a/solution.py
+++ b/solution.py
@@ -199,7 +199,7 @@
         top = prod[:512] + prod[512:]
         sbuf[p] = (top[:, :128] + top[:, 128:]).reshape(SCAN, 2, ROWS, 128)
 
-    chip, own = lax.div(me, 2), lax.rem(me, 2)
+    y, zl, own = lax.div(me, 8), lax.rem(lax.div(me, 2), 4), lax.rem(me, 2)
 
     def send(p, to, q):
         pltpu.make_async_remote_copy(
@@ -218,9 +218,9 @@
         def _():
             send(p, FIRST, q)
 
-        @pl.loop(1, 17)
+        @pl.loop(0, 16)
         def _(i):
-            to = lax.rem(chip + i, 16) * 2 + core
+            to = lax.rem(y + lax.div(i, 4), 4) * 8 + lax.rem(zl + 1 + i, 4) * 2 + core
             led = jnp.logical_and(p == 3, to == FIRST)
 
             @pl.when(jnp.logical_not(jnp.logical_or(to == me, led)))

time: 52.1 us -> 52.7 us (1.012)
  the two profiles are of different devices: /device:TPU:1 before, /device:TPU:8 now
where the time goes in v5:
time: 52.7 us; the launch traced here: 52.6 us
  Pallas kernels  51.9 us (98%)
  local copies, waits for them, and re-layouts  0.62 us (1%)
    pallas_call x1, Pallas kernels, local(): pl.pallas_call(kernel, out_shape=jax.ShapeDtypeStruct((2, BLOCK, N // (X...  51.9 us

profile of v5, /device:TPU:8, one launch (start us, length us, event | category | flops | bytes accessed | tf_op | source)
XLA Modules:
  0.0 52.6 jit_solution(2160766079575594777)
XLA Ops:
  0.0 51.9 %ptycho.1 = f32[2,32,64]{2,1,0:T(8,128)S(1)} custom-call(f32[4,32,1024]{2,1,0:T(8,128)} %x_hbm.1, s32[4,32,1024]{2,1,0:T(8,128)} %lab_hbm.1, f32[32,1024]{1,0:T(8,128)} %phase_hbm.1, bf16[2,1024,256]{2,1,0:T(8,128)(2,1)} %constant.8.clone.even_hbm, bf16[2,1024,512]{2,1,0:T(8,128)(2,1)} %constant.9.clone.odd_hbm, ...), custom_call_target="tpu_custom_call" | custom-call | tf_op jit(solution)/shard_map/ptycho/pallas_call | solution.py:399
  52.0 0.6 %copy.9 = f32[2,32,64]{2,1,0:T(8,128)} copy(f32[2,32,64]{2,1,0:T(8,128)S(1)} %ptycho.1) | data formatting | bytes 32768

commit v6 on v4

--- a/solution.py
+++ b/solution.py
@@ -220,7 +220,7 @@
 
         @pl.loop(1, 17)
         def _(i):
-            to = lax.rem(chip + i, 16) * 2 + core
+            to = lax.rem(chip + 8 * own + i, 16) * 2 + core
             led = jnp.logical_and(p == 3, to == FIRST)
 
             @pl.when(jnp.logical_not(jnp.logical_or(to == me, led)))

time: 52.1 us -> 52 us (level)
  no operation moved by 1% of the time
where the time goes in v6:
time: 52 us; the launch traced here: 51.7 us
  Pallas kernels  51.1 us (98%)
  local copies, waits for them, and re-layouts  0.62 us (1%)
    pallas_call x1, Pallas kernels, local(): pl.pallas_call(kernel, out_shape=jax.ShapeDtypeStruct((2, BLOCK, N // (X...  51.1 us

profile of v6, /device:TPU:1, one launch (start us, length us, event | category | flops | bytes accessed | tf_op | source)
XLA Modules:
  0.0 51.7 jit_solution(15190519197231960551)
XLA Ops:
  0.0 51.1 %ptycho.1 = f32[2,32,64]{2,1,0:T(8,128)S(1)} custom-call(f32[4,32,1024]{2,1,0:T(8,128)} %x_hbm.1, s32[4,32,1024]{2,1,0:T(8,128)} %lab_hbm.1, f32[32,1024]{1,0:T(8,128)} %phase_hbm.1, bf16[2,1024,256]{2,1,0:T(8,128)(2,1)} %constant.8.clone.even_hbm, bf16[2,1024,512]{2,1,0:T(8,128)(2,1)} %constant.9.clone.odd_hbm, ...), custom_call_target="tpu_custom_call" | custom-call | tf_op jit(solution)/shard_map/ptycho/pallas_call | solution.py:399
  51.1 0.6 %copy.9 = f32[2,32,64]{2,1,0:T(8,128)} copy(f32[2,32,64]{2,1,0:T(8,128)S(1)} %ptycho.1) | data formatting | bytes 32768

commit v7 on v6

--- a/solution.py
+++ b/solution.py
@@ -311,17 +311,16 @@
                 for q, part in enumerate(swap_bits(sums[e], (4, 2))):
                     psend[p, q, qh, e] = part
 
-        @pl.loop(1, X)
-        def _(j):
-            q = (x + j) % X
-            pltpu.make_async_remote_copy(
-                src_ref=psend.at[p, q],
-                dst_ref=precv.at[p, j - 1],
-                send_sem=psend_sem.at[p],
-                recv_sem=precv_sem.at[p],
-                device_id=(me, q * Z + z),
-                device_id_type=MESH,
-            ).start()
+            for j in range(1, X):
+                q = lax.rem(x + j, X)
+                pltpu.make_async_remote_copy(
+                    src_ref=psend.at[p, q, qh],
+                    dst_ref=precv.at[p, j - 1, qh],
+                    send_sem=psend_sem.at[p],
+                    recv_sem=precv_sem.at[p],
+                    device_id=(me, q * Z + z),
+                    device_id_type=MESH,
+                ).start()
 
     def sum_x(p):
         pltpu.make_async_copy(precv.at[p], precv.at[p], precv_sem.at[p]).wait()
@@ -354,14 +353,17 @@
         @pl.when(q < 6)
         def _():
             wait_sent(q)
+
+        @pl.when(jnp.logical_or(q == 3, q == 5))
+        def _():
+            sum_x(p - 1)
+
+        @pl.when(q < 6)
+        def _():
             send_chunk(q + 2)
 
         @pl.when(lax.rem(q, 2) == 1)
         def _():
-            @pl.when(jnp.logical_and(p > 0, p < 3))
-            def _():
-                sum_x(p - 1)
-
             row_part(p)
 
     sum_x(2)

time: 52 us -> 52.3 us (level); the launches traced: 51.7 us -> 51.3 us
  no operation moved by 1% of the time
where the time goes in v7:
time: 52.3 us; the launch traced here: 51.3 us
  Pallas kernels  50.7 us (97%)
  local copies, waits for them, and re-layouts  0.62 us (1%)
    pallas_call x1, Pallas kernels, local(): pl.pallas_call(kernel, out_shape=jax.ShapeDtypeStruct((2, BLOCK, N // (X...  50.7 us

profile of v7, /device:TPU:1, one launch (start us, length us, event | category | flops | bytes accessed | tf_op | source)
XLA Modules:
  0.0 51.3 jit_solution(15681138591122510195)
XLA Ops:
  0.0 50.7 %ptycho.1 = f32[2,32,64]{2,1,0:T(8,128)S(1)} custom-call(f32[4,32,1024]{2,1,0:T(8,128)} %x_hbm.1, s32[4,32,1024]{2,1,0:T(8,128)} %lab_hbm.1, f32[32,1024]{1,0:T(8,128)} %phase_hbm.1, bf16[2,1024,256]{2,1,0:T(8,128)(2,1)} %constant.8.clone.even_hbm, bf16[2,1024,512]{2,1,0:T(8,128)(2,1)} %constant.9.clone.odd_hbm, ...), custom_call_target="tpu_custom_call" | custom-call | tf_op jit(solution)/shard_map/ptycho/pallas_call | solution.py:401
  50.7 0.6 %copy.9 = f32[2,32,64]{2,1,0:T(8,128)} copy(f32[2,32,64]{2,1,0:T(8,128)S(1)} %ptycho.1) | data formatting | bytes 32768

commit v8 on v6

--- a/solution.py
+++ b/solution.py
@@ -242,6 +242,8 @@
     for h, (x0, x1, x2, x3) in enumerate(quarter):
         put((x0 + x2) - (x1 + x3), 256 + h * 128)
     column_part(1)
+    send_chunk(2)
+    send_chunk(3)
     for h, (x0, x1, x2, x3) in enumerate(quarter):
         put(x0 - x2, 512 + h * 128)
         put(x1 - x3, 768 + h * 128)
@@ -354,6 +356,9 @@
         @pl.when(q < 6)
         def _():
             wait_sent(q)
+
+        @pl.when(jnp.logical_and(q > 1, q < 6))
+        def _():
             send_chunk(q + 2)
 
         @pl.when(lax.rem(q, 2) == 1)

time: 52 us -> 52.4 us (level)
  no operation moved by 1% of the time
where the time goes in v8:
time: 52.4 us; the launch traced here: 51.7 us
  Pallas kernels  51.1 us (98%)
  local copies, waits for them, and re-layouts  0.62 us (1%)
    pallas_call x1, Pallas kernels, local(): pl.pallas_call(kernel, out_shape=jax.ShapeDtypeStruct((2, BLOCK, N // (X...  51.1 us

profile of v8, /device:TPU:1, one launch (start us, length us, event | category | flops | bytes accessed | tf_op | source)
XLA Modules:
  0.0 51.7 jit_solution(3070277606934373935)
XLA Ops:
  0.0 51.1 %ptycho.1 = f32[2,32,64]{2,1,0:T(8,128)S(1)} custom-call(f32[4,32,1024]{2,1,0:T(8,128)} %x_hbm.1, s32[4,32,1024]{2,1,0:T(8,128)} %lab_hbm.1, f32[32,1024]{1,0:T(8,128)} %phase_hbm.1, bf16[2,1024,256]{2,1,0:T(8,128)(2,1)} %constant.8.clone.even_hbm, bf16[2,1024,512]{2,1,0:T(8,128)(2,1)} %constant.9.clone.odd_hbm, ...), custom_call_target="tpu_custom_call" | custom-call | tf_op jit(solution)/shard_map/ptycho/pallas_call | solution.py:404
  51.1 0.6 %copy.9 = f32[2,32,64]{2,1,0:T(8,128)} copy(f32[2,32,64]{2,1,0:T(8,128)S(1)} %ptycho.1) | data formatting | bytes 32768
